TPU v7x, 32 devices: a whole 2x2x4 slice. The times are simulated.
32 devices in a mesh: groups: 2 (over y), dp: 4 (over z), tensor: 4 (over x, core).
Axes of the slice: x: 2, y: 2, z: 4, core: 2. Of those that a mesh axis runs over, the one named last changes fastest.
Arguments:
- queries: bfloat16 [2048, 5120], P(('groups', 'dp'), 'tensor'), parts along dimension 0, may hold values from -150 to 150
- suffix_keys: bfloat16 [2048, 1024], P(('groups', 'dp'), 'tensor'), parts along dimension 0, may hold values from -10 to 10
- suffix_values: bfloat16 [2048, 1024], P(('groups', 'dp'), 'tensor'), parts along dimension 0, may hold values from -6 to 6
- prefix_keys: bfloat16 [512, 1024], P(('groups', 'dp'), 'tensor'), parts along dimension 0, may hold values from -6 to 6
- prefix_values: bfloat16 [512, 1024], P(('groups', 'dp'), 'tensor'), parts along dimension 0, may hold values from -6 to 6
- grad_out: bfloat16 [2048, 5120], P(('groups', 'dp'), 'tensor'), parts along dimension 0, may hold values from -6 to 6
- parents: int32 [8], P('groups'), parts along dimension 0, may hold values from -1 to 2, as said below
- leaves: int32 [16], P(('groups', 'dp')), parts along dimension 0, may hold values from 0 to 3
- node_len: int32 [8], P('groups'), parts along dimension 0, may hold values from 1 to 64
Outputs:
- grad_queries: bfloat16 [2048, 5120], P(('groups', 'dp'), 'tensor'), parts along dimension 0
- grad_suffix_keys: bfloat16 [2048, 1024], P(('groups', 'dp'), 'tensor'), parts along dimension 0
- grad_suffix_values: bfloat16 [2048, 1024], P(('groups', 'dp'), 'tensor'), parts along dimension 0
- grad_prefix_keys: bfloat16 [512, 1024], P(('groups', 'dp'), 'tensor'), parts along dimension 0
- grad_prefix_values: bfloat16 [512, 1024], P(('groups', 'dp'), 'tensor'), parts along dimension 0
There are 2 independent parts, one for each index of `groups`. A program takes and returns all parts, laid end to end along the dimension named above; each array names one. Nothing has to cross between parts.
Inputs may be any that keep to these rules, and one draw needn't show every extreme that they name: parents[n] < n; a -1 marks the root of a tree.
All inputs are finite; a program needn't handle non-finite values.
Results may differ from a plain program's by a relative error of at most 0.0051.
Values may be sent and summed in bfloat16 or wider, within the bound.
A program may use at most 64 MiB of HBM per device.

v0:
```python
import jax
import jax.numpy as jnp
from jax import lax
from jax.sharding import PartitionSpec as P

HD = 128
BLK = 64
SUF = 128


def ancestry(leaves, parents):
    node_ids = jnp.arange(parents.shape[0], dtype=jnp.int32)

    def climb_step(position, running):
        on_path, current = running
        node_hot = current[:, None] == node_ids[None, :]
        upward = jnp.sum(jnp.where(node_hot, parents[None, :], 0), axis=1)
        current = jnp.where(jnp.any(node_hot, axis=1), upward, -1)
        return (on_path | node_hot, current)

    start_path = jnp.zeros((leaves.shape[0], parents.shape[0]), dtype=jnp.bool_)
    on_path, current = lax.fori_loop(0, parents.shape[0], climb_step, (start_path, leaves))
    return on_path


def dot_rows(left_side, right_side):
    return lax.dot_general(
        left_side, right_side, (((1,), (1,)), ((), ())), preferred_element_type=jnp.float32
    )


def dot_cols(left_side, right_side):
    return lax.dot_general(
        left_side, right_side, (((0,), (0,)), ((), ())), preferred_element_type=jnp.float32
    )


def head_split(rows_in):
    return rows_in.reshape(rows_in.shape[0], rows_in.shape[1] // HD, HD).transpose(1, 0, 2)


def stats_block(query_heads, grad_heads, key_rows, value_rows, allowed, running):
    kv_count = key_rows.shape[1] // HD
    group_size = query_heads.shape[0] // kv_count
    key_heads = head_split(key_rows)
    value_heads = head_split(value_rows)
    score_scale = HD ** (-0.5)

    def stats_per_head(inputs):
        query_one, grad_one, row_max, row_sum, row_dot, head_idx = inputs
        key_one = key_heads[head_idx // group_size]
        value_one = value_heads[head_idx // group_size]
        scores = dot_rows(query_one, key_one) * score_scale
        grad_p = dot_rows(grad_one, value_one)
        new_max = jnp.maximum(row_max, jnp.max(jnp.where(allowed, scores, -1e30), axis=1))
        shrink = jnp.exp(row_max - new_max)
        weights = jnp.where(allowed, jnp.exp(scores - new_max[:, None]), 0.0)
        return (
            new_max,
            row_sum * shrink + jnp.sum(weights, axis=1),
            row_dot * shrink + jnp.sum(weights * grad_p, axis=1),
        )

    row_max, row_sum, row_dot = running
    head_ids = jnp.arange(query_heads.shape[0], dtype=jnp.int32)
    return lax.map(stats_per_head, (query_heads, grad_heads, row_max, row_sum, row_dot, head_ids))


def backward_block(query_heads, grad_heads, log_total, row_delta, key_rows, value_rows, allowed):
    kv_count = key_rows.shape[1] // HD
    group_size = query_heads.shape[0] // kv_count
    key_heads = head_split(key_rows)
    value_heads = head_split(value_rows)
    score_scale = HD ** (-0.5)

    def backward_per_head(inputs):
        query_one, grad_one, total_one, delta_one, head_idx = inputs
        key_one = key_heads[head_idx // group_size]
        value_one = value_heads[head_idx // group_size]
        scores = dot_rows(query_one, key_one) * score_scale
        grad_p = dot_rows(grad_one, value_one)
        probs = jnp.where(allowed, jnp.exp(scores - total_one[:, None]), 0.0)
        probs_half = probs.astype(jnp.bfloat16)
        grad_s_half = (probs * (grad_p - delta_one[:, None])).astype(jnp.bfloat16)
        grad_q = score_scale * jnp.dot(grad_s_half, key_one, preferred_element_type=jnp.float32)
        grad_k = score_scale * dot_cols(grad_s_half, query_one)
        grad_v = dot_cols(probs_half, grad_one)
        return (grad_q, grad_k, grad_v)

    head_ids = jnp.arange(query_heads.shape[0], dtype=jnp.int32)
    grad_q, grad_k, grad_v = lax.map(
        backward_per_head, (query_heads, grad_heads, log_total, row_delta, head_ids)
    )
    key_count = key_rows.shape[0]
    grad_k = (
        grad_k.reshape(kv_count, group_size, key_count, HD)
        .sum(1)
        .transpose(1, 0, 2)
        .reshape(key_count, kv_count * HD)
    )
    grad_v = (
        grad_v.reshape(kv_count, group_size, key_count, HD)
        .sum(1)
        .transpose(1, 0, 2)
        .reshape(key_count, kv_count * HD)
    )
    return (grad_q, jnp.concatenate([grad_k, grad_v], axis=1))


def body(
    queries,
    suffix_keys,
    suffix_values,
    prefix_keys,
    prefix_values,
    grad_out,
    parents,
    leaves,
    node_len,
):
    row_count = queries.shape[0]
    head_count = queries.shape[1] // HD
    kv_width = suffix_keys.shape[1]
    node_total = parents.shape[0]
    on_path = ancestry(leaves, parents).astype(jnp.float32)
    node_ids = jnp.arange(node_total, dtype=jnp.int32)
    query_heads = head_split(queries)
    grad_heads = head_split(grad_out)
    row_ids = jnp.arange(row_count, dtype=jnp.int32)
    suffix_allowed = (row_ids[:, None] // SUF == row_ids[None, :] // SUF) & (
        row_ids[None, :] <= row_ids[:, None]
    )

    def prefix_allowed(key_count):
        slot_ids = jnp.arange(key_count, dtype=jnp.int32)
        node_hot = (slot_ids // BLK)[:, None] == node_ids[None, :]
        live_len = jnp.sum(jnp.where(node_hot, node_len[None, :], 0), axis=1)
        branch_sees = jnp.dot(on_path, node_hot.T.astype(jnp.float32)) > 0.5
        return jnp.repeat(branch_sees, SUF, axis=0) & (slot_ids % BLK < live_len)[None, :]

    start_stats = (
        jnp.full((head_count, row_count), -1e30, jnp.float32),
        jnp.zeros((head_count, row_count), jnp.float32),
        jnp.zeros((head_count, row_count), jnp.float32),
    )
    running = stats_block(
        query_heads, grad_heads, suffix_keys, suffix_values, suffix_allowed, start_stats
    )
    block_pair = (
        lax.all_gather(prefix_keys, "dp", axis=0, tiled=True),
        lax.all_gather(prefix_values, "dp", axis=0, tiled=True),
    )
    allowed = prefix_allowed(block_pair[0].shape[0])
    running = lax.cond(
        jnp.any(allowed),
        lambda current: stats_block(
            query_heads, grad_heads, block_pair[0], block_pair[1], allowed, current
        ),
        lambda current: current,
        running,
    )
    row_max, row_sum, row_dot = running
    log_total = row_max + jnp.log(row_sum)
    row_delta = row_dot / row_sum
    grad_q, suffix_grads = backward_block(
        query_heads, grad_heads, log_total, row_delta, suffix_keys, suffix_values, suffix_allowed
    )
    start_grads = (grad_q, jnp.zeros((node_total * BLK, 2 * kv_width), jnp.float32))
    fold_block_pair = (
        lax.all_gather(prefix_keys, "dp", axis=0, tiled=True),
        lax.all_gather(prefix_values, "dp", axis=0, tiled=True),
    )
    key_count = fold_block_pair[0].shape[0]
    fold_allowed = prefix_allowed(key_count)

    def accumulate(current):
        grad_add, grad_pair = backward_block(
            query_heads,
            grad_heads,
            log_total,
            row_delta,
            fold_block_pair[0],
            fold_block_pair[1],
            fold_allowed,
        )
        return (current[0] + grad_add, grad_pair)

    grad_q_total, summed = lax.cond(
        jnp.any(fold_allowed), accumulate, lambda current: current, start_grads
    )
    local_rows = prefix_keys.shape[0]
    everyone_rows = lax.psum(summed, "dp")
    own_rows = lax.dynamic_slice_in_dim(
        everyone_rows, lax.axis_index("dp") * local_rows, local_rows, 0
    )
    grad_queries = (
        grad_q_total.transpose(1, 0, 2).reshape(row_count, head_count * HD).astype(jnp.bfloat16)
    )
    return (
        grad_queries,
        suffix_grads[:, :kv_width].astype(jnp.bfloat16),
        suffix_grads[:, kv_width:].astype(jnp.bfloat16),
        own_rows[:, :kv_width].astype(jnp.bfloat16),
        own_rows[:, kv_width:].astype(jnp.bfloat16),
    )


def solution(mesh):
    placed = (
        P(("groups", "dp"), "tensor"),
        P(("groups", "dp"), "tensor"),
        P(("groups", "dp"), "tensor"),
        P(("groups", "dp"), "tensor"),
        P(("groups", "dp"), "tensor"),
        P(("groups", "dp"), "tensor"),
        P("groups"),
        P(("groups", "dp")),
        P("groups"),
    )
    return jax.shard_map(
        body,
        mesh=mesh,
        in_specs=placed,
        out_specs=(
            P(("groups", "dp"), "tensor"),
            P(("groups", "dp"), "tensor"),
            P(("groups", "dp"), "tensor"),
            P(("groups", "dp"), "tensor"),
            P(("groups", "dp"), "tensor"),
        ),
        check_vma=False,
    )
```

profile of v0, /device:TPU:0, one launch (start us, length us, event | category | flops | bytes accessed | tf_op | source)
XLA Modules:
  0.0 278.6 jit_solution(2085082913248521343)
XLA Ops:
  1.4 4.2 %while.93 = (s32[]{:T(128)}, pred[2,4]{1,0:T(4,128)(4,1)S(1)}, s32[2]{0:T(128)S(1)}, s32[4]{0:T(128)}, s32[]{:T(128)}, /*index=5*/s32[]{:T(128)}) while((s32[]{:T(128)}, pred[2,4]{1,0:T(4,128)(4,1)S(1)}, s32[2]{0:T(128)S(1)}, s32[4]{0:T(128)}, s32[]{:T(128)}, /*index=5*/s32[]{:T(128)}) %tuple.229), condition=%wide.region_3.4_spmd.clone, body=%wide.region_0.3_spmd.clone.sunk | while | flops 57 | bytes 155 | solution.py:22
  7.9 15.3 %all_gather.8 = bf16[256,256]{1,0:T(8,128)(2,1)S(1)} all-gather(bf16[64,256]{1,0:T(8,128)(2,1)} %param.26), channel_id=1, replica_groups=mesh['groups'=2,'dp'=4,'tensor'=4] {'dp'}, dimensions={0}, use_global_device_ids=true | all-gather | bytes 163840 | tf_op jit(solution)/shard_map/all_gather | solution.py:150
  23.2 13.7 %all_gather.9 = bf16[256,256]{1,0:T(8,128)(2,1)S(1)} all-gather(bf16[64,256]{1,0:T(8,128)(2,1)} %param.27), channel_id=1, replica_groups=mesh['groups'=2,'dp'=4,'tensor'=4] {'dp'}, dimensions={0}, use_global_device_ids=true | all-gather | bytes 163840 | tf_op jit(solution)/shard_map/all_gather | solution.py:151
  36.9 1.0 copy.109
  38.1 1.0 copy.111
  40.9 33.3 %while.92 = (s32[]{:T(128)}, f32[10,256]{1,0:T(8,128)S(1)}, f32[10,256]{1,0:T(8,128)S(1)}, f32[10,256]{1,0:T(8,128)S(1)}, bf16[10,256,128]{2,1,0:T(8,128)(2,1)S(...) while((s32[]{:T(128)}, f32[10,256]{1,0:T(8,128)S(1)}, ...), condition=%wide.region_10.11_spmd.clone.clone, body=%wide.region_6.10_spmd.clone.clone.sunk | while | flops 34800140 | bytes 1072445 | solution.py:66
  75.0 31.9 %conditional.2 = ((f32[10,256]{1,0:T(8,128)S(1)}, f32[10,256]{1,0:T(8,128)S(1)}, f32[10,256]{1,0:T(8,128)S(1)})) conditional(s32[]{:T(128)} %convert_element_type.60, (f32[10,256]{1,0:T(8,128)S(1)}, f32[10,256]{1,0:T(8,128)S(1)}, f32[10,256]{1,0:T(8,128)S(1)}) %tuple.101, (bf16[256,256]{1,0:T(8,128)(2,1)S(1)}, ...), branch_computations={%region_11.12_spmd.clone, %region_12.18_spmd.clone} | conditional | flops 34211084 | bytes 1990225 | solution.py:154
  75.4 31.5 %while.89 = (s32[]{:T(128)}, f32[10,256]{1,0:T(8,128)S(1)}, f32[10,256]{1,0:T(8,128)S(1)}, f32[10,256]{1,0:T(8,128)S(1)}, f32[10,256]{1,0:T(8,128)S(1)}, /*index...) while((s32[]{:T(128)}, f32[10,256]{1,0:T(8,128)S(1)}, ...), condition=%wide.region_17.17_spmd, body=%wide.region_13.16_spmd.sunk | while | flops 34211084 | bytes 1273185 | solution.py:66
  107.0 74.7 %while.91 = (s32[]{:T(128)}, f32[10,256,128]{2,1,0:T(8,128)S(1)}, f32[10,256,128]{2,1,0:T(8,128)}, f32[10,256,128]{2,1,0:T(8,128)}, bf16[10,256,128]{2,1,0:T(8,1...) while((s32[]{:T(128)}, f32[10,256,128]{2,1,0:T(8,128)S(1)}, ...), condition=%wide.region_19.20_spmd.clone, body=%wide.region_18.19_spmd.clone.sunk | while | flops 84606992 | bytes 2042189 | solution.py:91
  109.6 1.1 fusion.166
  110.6 1.0 fusion.167
  112.8 1.7 fusion.169
  117.0 1.1 fusion.166
  118.1 1.0 fusion.167
  120.2 1.7 fusion.169
  124.5 1.1 fusion.166
  125.6 1.0 fusion.167
  127.7 1.7 fusion.169
  132.0 1.1 fusion.166
  133.1 1.0 fusion.167
  135.2 1.7 fusion.169
  139.5 1.1 fusion.166
  140.5 1.0 fusion.167
  142.6 1.7 fusion.169
  146.9 1.1 fusion.166
  148.0 1.0 fusion.167
  150.1 1.7 fusion.169
  154.4 1.1 fusion.166
  155.5 1.0 fusion.167
  157.6 1.7 fusion.169
  161.9 1.1 fusion.166
  162.9 1.0 fusion.167
  165.1 1.7 fusion.169
  169.4 1.1 fusion.166
  170.4 1.0 fusion.167
  172.5 1.7 fusion.169
  176.8 1.1 fusion.166
  177.9 1.0 fusion.167
  180.0 1.7 fusion.169
  181.7 1.4 reduce_sum.116
  184.0 1.4 reduce_sum.115
  186.3 63.3 %conditional.3 = (f32[10,256,128]{2,1,0:T(8,128)S(1)}, f32[256,512]{0,1:T(8,128)S(1)}) conditional(s32[]{:T(128)} %convert_element_type.60, f32[10,256,128]{2,1,0:T(8,128)S(1)} %get-tuple-element.749, (bf16[256,256]{1,0:T(8,128)(2,1)S(1)}, bf16[256,256]{1,0:T(8,128)(2,1)S(1)}, bf16[10,256,128]{1,2,0:T(8,128)(2,1)S(1)}, f32[10,256]{1,0:T(8,128)S(1)}, ...), branch_computations={%region_20.21_spmd, %region_21.26_spmd} | conditional | flops 85393424 | bytes 22291044 | solution.py:188
  186.6 56.4 %while.90 = (s32[]{:T(128)}, f32[10,256,128]{2,1,0:T(8,128)}, f32[10,256,128]{2,1,0:T(8,128)}, f32[10,256,128]{2,1,0:T(8,128)}, bf16[10,256,128]{1,2,0:T(8,128)(...) while((s32[]{:T(128)}, f32[10,256,128]{2,1,0:T(8,128)}, ...), condition=%wide.region_23.23_spmd, body=%wide.region_22.22_spmd.sunk | while | flops 84410384 | bytes 2105677 | solution.py:91
  243.0 1.5 reduce_sum.110
  245.5 1.9 copy.104
  248.2 1.1 pad_maximum_fusion
  249.8 1.1 copy.133
  251.1 26.8 %all-reduce.1 = bf16[256,512]{1,0:T(8,128)(2,1)S(1)} all-reduce(f32[256,512]{1,0:T(8,128)S(1)} %copy.132), channel_id=1, replica_groups=mesh['groups'=2,'dp'=4,'tensor'=4] {'dp'}, use_global_device_ids=true, to_apply=%region_28.29 | all-reduce | flops 131072 | bytes 786432 | tf_op jit(solution)/shard_map/psum | solution.py:192
  (393 shorter events, 94.8 us)
Async XLA Ops:
  0.6 38.6 %copy-start.8 = (bf16[256,1280]{1,0:T(8,128)(2,1)S(1)}, bf16[256,1280]{1,0:T(8,128)(2,1)}, u32[]{:S(2)}) copy-start(bf16[256,1280]{1,0:T(8,128)(2,1)} %param.23) | copy-start | bytes 1966084
  23.2 51.0 %copy-start.4 = (bf16[256,256]{1,0:T(8,128)(2,1)}, bf16[256,256]{1,0:T(8,128)(2,1)S(1)}, u32[]{:S(2)}) copy-start(bf16[256,256]{1,0:T(8,128)(2,1)S(1)} %all_gather.8) | copy-start | bytes 393220
  36.9 37.3 %copy-start.6 = (bf16[256,256]{1,0:T(8,128)(2,1)}, bf16[256,256]{1,0:T(8,128)(2,1)S(1)}, u32[]{:S(2)}) copy-start(bf16[256,256]{1,0:T(8,128)(2,1)S(1)} %all_gather.9) | copy-start | bytes 393220
  39.2 1.1 copy-start.9
  74.1 0.7 copy-start
  74.1 0.9 copy-start.1
  183.1 3.2 %copy-start.5 = (bf16[256,256]{1,0:T(8,128)(2,1)S(1)}, bf16[256,256]{1,0:T(8,128)(2,1)}, u32[]{:S(2)}) copy-start(bf16[256,256]{1,0:T(8,128)(2,1)} %copy-done.4) | copy-start | bytes 393220
  183.1 3.2 %copy-start.7 = (bf16[256,256]{1,0:T(8,128)(2,1)S(1)}, bf16[256,256]{1,0:T(8,128)(2,1)}, u32[]{:S(2)}) copy-start(bf16[256,256]{1,0:T(8,128)(2,1)} %copy-done.6) | copy-start | bytes 393220
  243.0 1.7 copy-start.2
  245.4 3.8 %copy-start.3 = (f32[10,256,128]{2,1,0:T(8,128)S(1)}, f32[10,256,128]{2,1,0:T(8,128)}, u32[]{:S(2)}) copy-start(f32[10,256,128]{2,1,0:T(8,128)} %get-tuple-element.722) | copy-start | bytes 3932164 | tf_op jit(solution)/shard_map/cond
where the time goes:
time: 281 us; the launch traced here: 279 us
  matrix products  89.4 us (32%)
  loops' own time  77.8 us (28%)
  blocking collectives  55.8 us (20%)
  local copies, waits for them, and re-layouts  39.2 us (14%)
  other arithmetic  14.8 us (5%)
    dot_general x40, matrix products, dot_cols(): lax.dot_general(left_side, right_side, (((0,), (0,)), ((), ())), preferre...  43.6 us
    another operation x2, loops' own time, backward_block(): lax.map(backward_per_head, (query_heads, grad_heads, log_total, row_delta...  39.9 us
    another operation x2, loops' own time, stats_block(): lax.map(stats_per_head, (query_heads, grad_heads, row_max, row_sum, row_d...  37.8 us
    dot_general x80, matrix products, dot_rows(): lax.dot_general(left_side, right_side, (((1,), (1,)), ((), ())), preferre...  35.5 us
    psum x1, blocking collectives, body(): everyone_rows = lax.psum(summed, 'dp')  26.8 us
    dynamic_slice x70, local copies, waits for them, and re-layouts, stats_block(): lax.map(stats_per_head, (query_heads, grad_heads, row_max, row_sum, row_d...  23.7 us
    all_gather x1, blocking collectives, body(): lax.all_gather(prefix_keys, 'dp', axis=0, tiled=True)  15.3 us
    all_gather x1, blocking collectives, body(): lax.all_gather(prefix_values, 'dp', axis=0, tiled=True)  13.7 us

commit v1 on v0

v1 whole, which is shorter than its diff:
```python
import functools
import math

import jax
import jax.numpy as jnp
from jax import lax
from jax.experimental import pallas as pl
from jax.experimental.pallas import tpu as pltpu
from jax.sharding import PartitionSpec as P

HD = 128
BLK = 64
SUF = 128
SCALE = HD ** -0.5
EXP_SCALE = SCALE * math.log2(math.e)
LOW = -1e30
MESH = pl.DeviceIdType.MESH


def dot_nt(left, right):
    return lax.dot_general(
        left, right, (((1,), (1,)), ((), ())), preferred_element_type=jnp.float32
    )


def dot_nn(left, right):
    return jnp.dot(left, right, preferred_element_type=jnp.float32)


def over(count, step, start):
    if count == 1:
        return step(0, start)
    return lax.fori_loop(0, count, step, start)


def kernel(
    n,
    q_hbm, ks_hbm, vs_hbm, kp_hbm, vp_hbm, g_hbm, parents_ref, leaves_ref, len_ref,
    gq_ref, gks_ref, gvs_ref, gkp_ref, gvp_ref,
    q, g, ks, vs, kp, vp, w_s, gp_s, p_half, ds_half, bias, stats, own, sbuf, rbuf,
    in_sem, k_send, k_recv, v_send, v_recv, r_send, r_recv,
):
    rows, width = q.shape
    heads = width // HD
    kv = ks.shape[1] // HD
    group = heads // kv
    nb = rows // SUF
    local = kp_hbm.shape[0]
    slots = n * local
    chunk = min(slots, 256)
    chunks = slots // chunk
    me = lax.axis_index("dp")
    peers = [lax.rem(me + j, n) for j in range(1, n)]

    barrier = pltpu.get_barrier_semaphore()
    for peer in peers:
        pl.semaphore_signal(barrier, inc=1, device_id={"dp": peer}, device_id_type=MESH)

    part = group * HD
    loads = [
        pltpu.make_async_copy(ks_hbm, ks, in_sem.at[0]),
        pltpu.make_async_copy(vs_hbm, vs, in_sem.at[1]),
    ]
    for m in range(kv):
        cols = pl.ds(m * part, part)
        loads.append(pltpu.make_async_copy(q_hbm.at[:, cols], q.at[:, cols], in_sem.at[4 + 2 * m]))
        loads.append(pltpu.make_async_copy(g_hbm.at[:, cols], g.at[:, cols], in_sem.at[5 + 2 * m]))
    mine = pl.ds(pl.multiple_of(me * local, local), local)
    own_copies = [
        pltpu.make_async_copy(kp_hbm, kp.at[mine], in_sem.at[2]),
        pltpu.make_async_copy(vp_hbm, vp.at[mine], in_sem.at[3]),
    ]
    for copy in loads + own_copies:
        copy.start()

    pl.semaphore_wait(barrier, n - 1)
    gathers = []
    for src, dst, send, recv in ((kp_hbm, kp, k_send, k_recv), (vp_hbm, vp, v_send, v_recv)):
        for j, peer in enumerate(peers):
            copy = pltpu.make_async_remote_copy(
                src_ref=src, dst_ref=dst.at[mine], send_sem=send.at[j], recv_sem=recv.at[j],
                device_id={"dp": peer}, device_id_type=MESH,
            )
            copy.start()
            gathers.append(copy)

    nodes = len_ref.shape[0]
    place = lax.broadcasted_iota(jnp.int32, (BLK, SUF), 0)
    for b in range(nb):
        current = leaves_ref[b]
        for node in reversed(range(nodes)):
            hit = current == node
            live = jnp.where(hit, len_ref[node], 0)
            current = jnp.where(hit, parents_ref[node], current)
            bias[node * BLK:(node + 1) * BLK, b * SUF:(b + 1) * SUF] = jnp.where(
                place < live, 0.0, LOW
            )

    causal = lax.broadcasted_iota(jnp.int32, (SUF, SUF), 0) <= lax.broadcasted_iota(
        jnp.int32, (SUF, SUF), 1
    )
    hcol = lambda h: slice(h * HD, (h + 1) * HD)
    brow = lambda b: slice(b * SUF, (b + 1) * SUF)

    loads[0].wait()
    loads[1].wait()
    for h in range(heads):
        m = h // group
        if h % group == 0:
            loads[2 + 2 * m].wait()
            loads[3 + 2 * m].wait()
        for b in range(nb):
            s = dot_nt(ks[brow(b), hcol(m)], q[brow(b), hcol(h)])
            s = jnp.where(causal, s, LOW)
            gp = dot_nt(vs[brow(b), hcol(m)], g[brow(b), hcol(h)])
            top = jnp.max(s, axis=0, keepdims=True)
            w = jnp.exp2((s - top) * EXP_SCALE)
            w_s[h, :, brow(b)] = w
            gp_s[h, :, brow(b)] = gp
            stats[h, 0:1, brow(b)] = top
            stats[h, 1:2, brow(b)] = jnp.sum(w, axis=0, keepdims=True)
            stats[h, 2:3, brow(b)] = jnp.sum(w * gp, axis=0, keepdims=True)

    for copy in own_copies:
        copy.wait()
    for copy in gathers:
        copy.wait_recv()

    sends = []
    for m in range(kv):
        for i in range(group):
            h = m * group + i

            def at(c):
                if chunks == 1:
                    return slice(0, chunk)
                return pl.ds(pl.multiple_of(c * chunk, chunk), chunk)

            def scores(c):
                return dot_nt(kp[at(c), hcol(m)], q[:, hcol(h)]) + bias[at(c), :]

            def grads(c):
                return dot_nt(vp[at(c), hcol(m)], g[:, hcol(h)])

            if chunks == 1:
                only_s, only_g = scores(0), grads(0)
                scores, grads = (lambda c: only_s), (lambda c: only_g)
            top_s = stats[h, 0:1, :]
            top = over(
                chunks,
                lambda c, t: jnp.maximum(t, jnp.max(scores(c), axis=0, keepdims=True)),
                top_s,
            )
            shrink = jnp.exp2((top_s - top) * EXP_SCALE)
            weights = lambda c: jnp.exp2((scores(c) - top) * EXP_SCALE)
            if chunks == 1:
                only_w = weights(0)
                weights = lambda c: only_w

            def add_up(c, sums):
                w = weights(c)
                return (
                    sums[0] + jnp.sum(w, axis=0, keepdims=True),
                    sums[1] + jnp.sum(w * grads(c), axis=0, keepdims=True),
                )

            total, dotted = over(
                chunks, add_up, (stats[h, 1:2, :] * shrink, stats[h, 2:3, :] * shrink)
            )
            inverse = 1.0 / total
            delta = dotted * inverse
            stats[h, 3:4, :] = shrink * inverse
            stats[h, 4:5, :] = delta

            def finish(c, nothing):
                probs = weights(c) * inverse
                cols = slice(i * rows, (i + 1) * rows)
                p_half[m, at(c), cols] = probs.astype(jnp.bfloat16)
                ds_half[m, at(c), cols] = (probs * (grads(c) - delta)).astype(jnp.bfloat16)
                return nothing

            over(chunks, finish, 0)

        q_all = jnp.concatenate([q[:, hcol(m * group + i)] for i in range(group)], axis=0)
        g_all = jnp.concatenate([g[:, hcol(m * group + i)] for i in range(group)], axis=0)

        def reduce_node(d, nothing):
            at_d = pl.ds(pl.multiple_of(d * local, local), local)
            put(at_d, d, dot_nn(p_half[m, at_d, :], g_all), dot_nn(ds_half[m, at_d, :], q_all))
            return nothing

        def put(at_d, d, grad_v, grad_k):
            grad_k = grad_k * SCALE
            own[m, 0, at_d, :] = grad_k
            own[m, 1, at_d, :] = grad_v
            sbuf[m, d, 0] = grad_k.astype(jnp.bfloat16)
            sbuf[m, d, 1] = grad_v.astype(jnp.bfloat16)

        if chunks == 1:
            grad_v = dot_nn(p_half[m], g_all)
            grad_k = dot_nn(ds_half[m], q_all)
            for d in range(n):
                at_d = slice(d * local, (d + 1) * local)
                put(at_d, d, grad_v[at_d], grad_k[at_d])
        else:
            lax.fori_loop(0, n, reduce_node, 0)
        for j, peer in enumerate(peers):
            copy = pltpu.make_async_remote_copy(
                src_ref=sbuf.at[m, peer], dst_ref=rbuf.at[m, j],
                send_sem=r_send.at[m, j], recv_sem=r_recv.at[m, j],
                device_id={"dp": peer}, device_id_type=MESH,
            )
            copy.start()
            sends.append(copy)

    for m in range(kv):
        kp_t = kp[:, hcol(m)].T
        ks_t = [ks[brow(b), hcol(m)].T for b in range(nb)]
        p_parts = [[] for b in range(nb)]
        d_parts = [[] for b in range(nb)]
        for i in range(group):
            h = m * group + i
            probs = w_s[h] * stats[h, 3:4, :]
            ds = (probs * (gp_s[h] - stats[h, 4:5, :])).astype(jnp.bfloat16)
            probs = probs.astype(jnp.bfloat16)
            grad_q = dot_nn(kp_t, ds_half[m, :, i * rows:(i + 1) * rows])
            for b in range(nb):
                p_parts[b].append(probs[:, brow(b)])
                d_parts[b].append(ds[:, brow(b)])
                both = grad_q[:, brow(b)] + dot_nn(ks_t[b], ds[:, brow(b)])
                gq_ref[brow(b), hcol(h)] = (both * SCALE).T.astype(jnp.bfloat16)
        for b in range(nb):
            q_all = jnp.concatenate([q[brow(b), hcol(m * group + i)] for i in range(group)], axis=0)
            g_all = jnp.concatenate([g[brow(b), hcol(m * group + i)] for i in range(group)], axis=0)
            grad_v = dot_nn(jnp.concatenate(p_parts[b], axis=1), g_all)
            grad_k = dot_nn(jnp.concatenate(d_parts[b], axis=1), q_all) * SCALE
            gks_ref[brow(b), hcol(m)] = grad_k.astype(jnp.bfloat16)
            gvs_ref[brow(b), hcol(m)] = grad_v.astype(jnp.bfloat16)

    for copy in sends:
        copy.wait_recv()
    for m in range(kv):
        for which, out in ((0, gkp_ref), (1, gvp_ref)):
            summed = own[m, which, mine, :]
            for j in range(n - 1):
                summed = summed + rbuf[m, j, which].astype(jnp.float32)
            out[:, hcol(m)] = summed.astype(jnp.bfloat16)
    for copy in gathers + sends:
        copy.wait_send()


def body(n, queries, suffix_keys, suffix_values, prefix_keys, prefix_values, grad_out,
         parents, leaves, node_len):
    rows, width = queries.shape
    kv_width = suffix_keys.shape[1]
    heads, kv = width // HD, kv_width // HD
    group = heads // kv
    local = prefix_keys.shape[0]
    slots = n * local
    half, full = jnp.bfloat16, jnp.float32
    any_spec = pl.BlockSpec(memory_space=pl.ANY)
    smem = pl.BlockSpec(memory_space=pltpu.SMEM)
    vmem = pl.BlockSpec(memory_space=pltpu.VMEM)
    flops = 10 * rows * heads * HD * (slots + SUF)
    return pl.pallas_call(
        functools.partial(kernel, n),
        out_shape=(
            jax.ShapeDtypeStruct((rows, width), half),
            jax.ShapeDtypeStruct((rows, kv_width), half),
            jax.ShapeDtypeStruct((rows, kv_width), half),
            jax.ShapeDtypeStruct((local, kv_width), half),
            jax.ShapeDtypeStruct((local, kv_width), half),
        ),
        in_specs=[any_spec] * 6 + [smem] * 3,
        out_specs=(vmem,) * 5,
        scratch_shapes=[
            pltpu.VMEM((rows, width), half),
            pltpu.VMEM((rows, width), half),
            pltpu.VMEM((rows, kv_width), half),
            pltpu.VMEM((rows, kv_width), half),
            pltpu.VMEM((slots, kv_width), half),
            pltpu.VMEM((slots, kv_width), half),
            pltpu.VMEM((heads, SUF, rows), full),
            pltpu.VMEM((heads, SUF, rows), full),
            pltpu.VMEM((kv, slots, group * rows), half),
            pltpu.VMEM((kv, slots, group * rows), half),
            pltpu.VMEM((slots, rows), full),
            pltpu.VMEM((heads, 8, rows), full),
            pltpu.VMEM((kv, 2, slots, HD), full),
            pltpu.VMEM((kv, n, 2, local, HD), half),
            pltpu.VMEM((kv, n - 1, 2, local, HD), half),
            pltpu.SemaphoreType.DMA((4 + 2 * kv,)),
            pltpu.SemaphoreType.DMA((n - 1,)),
            pltpu.SemaphoreType.DMA((n - 1,)),
            pltpu.SemaphoreType.DMA((n - 1,)),
            pltpu.SemaphoreType.DMA((n - 1,)),
            pltpu.SemaphoreType.DMA((kv, n - 1)),
            pltpu.SemaphoreType.DMA((kv, n - 1)),
        ],
        compiler_params=pltpu.CompilerParams(
            collective_id=0, has_side_effects=True, vmem_limit_bytes=48 * 1024 * 1024
        ),
        cost_estimate=pl.CostEstimate(
            flops=flops, bytes_accessed=8 * rows * width, transcendentals=rows * heads * (slots + SUF)
        ),
    )(queries, suffix_keys, suffix_values, prefix_keys, prefix_values, grad_out,
      parents, leaves, node_len)


def solution(mesh):
    rows_cols = P(("groups", "dp"), "tensor")
    return jax.shard_map(
        functools.partial(body, mesh.shape["dp"]),
        mesh=mesh,
        in_specs=(rows_cols,) * 6 + (P("groups"), P(("groups", "dp")), P("groups")),
        out_specs=(rows_cols,) * 5,
        check_vma=False,
    )
```

time: 281 us -> 31.7 us (0.11)
  matrix products: 89.4 us -> 0 us
  loops' own time: 77.8 us -> 0 us
  blocking collectives: 55.8 us -> 0 us
  local copies, waits for them, and re-layouts: 39.2 us -> 10.8 us
  Pallas kernels: 0 us -> 19.8 us
  other arithmetic: 14.8 us -> 0 us
    dot_general x141 -> x0, matrix products: 89.4 us -> none  [the longest x40 43.6 us: dot_cols(): lax.dot_general(left_side, right_side, (((0,), (0,)), ((), ())), preferre...]
    another operation x7 -> x0, loops' own time: 77.8 us -> none  [the longest x2 39.9 us: backward_block(): lax.map(backward_per_head, (query_heads, grad_heads, log_total, row_delta...]
    all_gather x2 -> x0, blocking collectives: 29 us -> none  [the longest x1 15.3 us: body(): lax.all_gather(prefix_keys, 'dp', axis=0, tiled=True)]
    psum x1 -> x0, blocking collectives: 26.8 us -> none  [body(): everyone_rows = lax.psum(summed, 'dp')]
    dynamic_slice x70 -> x0, local copies, waits for them, and re-layouts: 23.7 us -> none  [stats_block(): lax.map(stats_per_head, (query_heads, grad_heads, row_max, row_sum, row_d...]
    pallas_call x0 -> x1, Pallas kernels: none -> 19.8 us  [body(): pl.pallas_call(functools.partial(kernel, n), out_shape=(jax.ShapeDtypeStr...]
    reduce_sum x29 -> x0, other arithmetic: 11.3 us -> none  [the longest x4 3.35 us: climb_step(): upward = jnp.sum(jnp.where(node_hot, parents[None, :], 0), axis=1)]
    unnamed x28 -> x23, local copies, waits for them, and re-layouts: 8.11 us -> 10.8 us
where the time goes in v1:
time: 31.7 us; the launch traced here: 31.3 us
  Pallas kernels  19.8 us (62%)
  local copies, waits for them, and re-layouts  10.8 us (34%)
  between operations  0.66 us (2%)
    pallas_call x1, Pallas kernels, body(): pl.pallas_call(functools.partial(kernel, n), out_shape=(jax.ShapeDtypeStr...  19.8 us
    unnamed x23, local copies, waits for them, and re-layouts  10.8 us

profile of v1, /device:TPU:0, one launch (start us, length us, event | category | flops | bytes accessed | tf_op | source)
XLA Modules:
  0.0 31.3 jit_solution(1780062078585266401)
XLA Ops:
  0.6 0.0 copy-start
  0.6 1.1 %copy-done = bf16[256,1280]{1,0:T(8,128)(2,1)S(1)} copy-done((bf16[256,1280]{1,0:T(8,128)(2,1)S(1)}, bf16[256,1280]{1,0:T(8,128)(2,1)}, u32[]{:S(2)}) %copy-start) | copy-done | bytes 655384
  1.7 0.0 copy-start.1
  1.7 1.1 %copy-done.1 = bf16[256,1280]{1,0:T(8,128)(2,1)S(1)} copy-done((bf16[256,1280]{1,0:T(8,128)(2,1)S(1)}, bf16[256,1280]{1,0:T(8,128)(2,1)}, u32[]{:S(2)}) %copy-start.1) | copy-done | bytes 655384
  2.8 0.0 copy-start.2
  2.8 0.9 %copy-done.2 = bf16[256,256]{1,0:T(8,128)(2,1)S(1)} copy-done((bf16[256,256]{1,0:T(8,128)(2,1)S(1)}, bf16[256,256]{1,0:T(8,128)(2,1)}, u32[]{:S(2)}) %copy-start.2) | copy-done | bytes 131096
  3.7 0.0 copy-start.3
  3.7 0.9 %copy-done.3 = bf16[256,256]{1,0:T(8,128)(2,1)S(1)} copy-done((bf16[256,256]{1,0:T(8,128)(2,1)S(1)}, bf16[256,256]{1,0:T(8,128)(2,1)}, u32[]{:S(2)}) %copy-start.3) | copy-done | bytes 131096
  4.6 0.0 copy-start.4
  4.6 0.8 %copy-done.4 = bf16[64,256]{1,0:T(8,128)(2,1)S(1)} copy-done((bf16[64,256]{1,0:T(8,128)(2,1)S(1)}, bf16[64,256]{1,0:T(8,128)(2,1)}, u32[]{:S(2)}) %copy-start.4) | copy-done | bytes 32792
  5.4 0.0 copy-start.5
  5.4 0.8 %copy-done.5 = bf16[64,256]{1,0:T(8,128)(2,1)S(1)} copy-done((bf16[64,256]{1,0:T(8,128)(2,1)S(1)}, bf16[64,256]{1,0:T(8,128)(2,1)}, u32[]{:S(2)}) %copy-start.5) | copy-done | bytes 32792
  6.1 0.0 copy-start.6
  6.1 0.7 %copy-done.6 = s32[4]{0:T(128)S(1)} copy-done((s32[4]{0:T(128)S(1)}, s32[4]{0:T(128)}, u32[]{:S(2)}) %copy-start.6) | copy-done | bytes 40
  6.8 0.0 copy-start.7
  6.8 0.7 %copy-done.7 = s32[2]{0:T(128)S(1)} copy-done((s32[2]{0:T(128)S(1)}, s32[2]{0:T(128)}, u32[]{:S(2)}) %copy-start.7) | copy-done | bytes 32
  7.4 0.0 copy-start.8
  7.5 0.7 %copy-done.8 = s32[4]{0:T(128)S(1)} copy-done((s32[4]{0:T(128)S(1)}, s32[4]{0:T(128)}, u32[]{:S(2)}) %copy-start.8) | copy-done | bytes 40
  8.1 19.8 %shard_map.128 = (bf16[256,1280]{1,0:T(8,128)(2,1)S(1)}, bf16[256,256]{1,0:T(8,128)(2,1)S(1)}, bf16[256,256]{1,0:T(8,128)(2,1)S(1)}, bf16[64,256]{1,0:T(8,128)(2,1)S(1)}, bf16[64,256]{1,0:T(8,128)(2,1)S(1)}) custom-call(bf16[256,1280]{1,0:T(8,128)(2,1)S(1)} %copy-done, bf16[256,256]{1,0:T(8,128)(2,1)S(1)} %copy-done.2, bf16[256,256]{1,0:T(8,128)(2,1)S(1)} %copy-done.3, ...), custom_call_target="tpu_custom_call" | custom-call | flops 1258291200 | bytes 2621440 | tf_op jit(solution)/shard_map/pallas_call | solution.py:265
  27.9 0.8 %copy.19 = bf16[256,1280]{1,0:T(8,128)(2,1)} copy(bf16[256,1280]{1,0:T(8,128)(2,1)S(1)} %get-tuple-element.10) | data formatting | bytes 1310720
  28.8 0.7 %copy.20 = bf16[256,256]{1,0:T(8,128)(2,1)} copy(bf16[256,256]{1,0:T(8,128)(2,1)S(1)} %get-tuple-element.11) | data formatting | bytes 262144
  29.4 0.7 %copy.21 = bf16[256,256]{1,0:T(8,128)(2,1)} copy(bf16[256,256]{1,0:T(8,128)(2,1)S(1)} %get-tuple-element.12) | data formatting | bytes 262144
  30.1 0.6 %copy.22 = bf16[64,256]{1,0:T(8,128)(2,1)} copy(bf16[64,256]{1,0:T(8,128)(2,1)S(1)} %get-tuple-element.13) | data formatting | bytes 65536
  30.7 0.6 %copy.23 = bf16[64,256]{1,0:T(8,128)(2,1)} copy(bf16[64,256]{1,0:T(8,128)(2,1)S(1)} %get-tuple-element.14) | data formatting | bytes 65536
Async XLA Ops:
  0.6 1.1 %copy-start = (bf16[256,1280]{1,0:T(8,128)(2,1)S(1)}, bf16[256,1280]{1,0:T(8,128)(2,1)}, u32[]{:S(2)}) copy-start(bf16[256,1280]{1,0:T(8,128)(2,1)} %q_hbm.1) | copy-start | bytes 1966084
  1.7 1.1 %copy-start.1 = (bf16[256,1280]{1,0:T(8,128)(2,1)S(1)}, bf16[256,1280]{1,0:T(8,128)(2,1)}, u32[]{:S(2)}) copy-start(bf16[256,1280]{1,0:T(8,128)(2,1)} %g_hbm.1) | copy-start | bytes 1966084
  2.8 0.9 %copy-start.2 = (bf16[256,256]{1,0:T(8,128)(2,1)S(1)}, bf16[256,256]{1,0:T(8,128)(2,1)}, u32[]{:S(2)}) copy-start(bf16[256,256]{1,0:T(8,128)(2,1)} %ks_hbm.1) | copy-start | bytes 393220
  3.7 0.9 %copy-start.3 = (bf16[256,256]{1,0:T(8,128)(2,1)S(1)}, bf16[256,256]{1,0:T(8,128)(2,1)}, u32[]{:S(2)}) copy-start(bf16[256,256]{1,0:T(8,128)(2,1)} %vs_hbm.1) | copy-start | bytes 393220
  4.6 0.8 %copy-start.4 = (bf16[64,256]{1,0:T(8,128)(2,1)S(1)}, bf16[64,256]{1,0:T(8,128)(2,1)}, u32[]{:S(2)}) copy-start(bf16[64,256]{1,0:T(8,128)(2,1)} %kp_hbm.1) | copy-start | bytes 98308
  5.4 0.8 %copy-start.5 = (bf16[64,256]{1,0:T(8,128)(2,1)S(1)}, bf16[64,256]{1,0:T(8,128)(2,1)}, u32[]{:S(2)}) copy-start(bf16[64,256]{1,0:T(8,128)(2,1)} %vp_hbm.1) | copy-start | bytes 98308
  6.1 0.7 %copy-start.6 = (s32[4]{0:T(128)S(1)}, s32[4]{0:T(128)}, u32[]{:S(2)}) copy-start(s32[4]{0:T(128)} %parents_ref.1) | copy-start | bytes 52
  6.8 0.7 %copy-start.7 = (s32[2]{0:T(128)S(1)}, s32[2]{0:T(128)}, u32[]{:S(2)}) copy-start(s32[2]{0:T(128)} %leaves_ref.1) | copy-start | bytes 28
  7.4 0.7 %copy-start.8 = (s32[4]{0:T(128)S(1)}, s32[4]{0:T(128)}, u32[]{:S(2)}) copy-start(s32[4]{0:T(128)} %len_ref.1) | copy-start | bytes 52

commit v2 on v1

--- a/solution.py
+++ b/solution.py
@@ -14,6 +14,7 @@
 SCALE = HD ** -0.5
 EXP_SCALE = SCALE * math.log2(math.e)
 LOW = -1e30
+LIMIT = 63 * 1024 * 1024
 MESH = pl.DeviceIdType.MESH
 
 
@@ -35,10 +36,11 @@
 
 def kernel(
     n,
-    q_hbm, ks_hbm, vs_hbm, kp_hbm, vp_hbm, g_hbm, parents_ref, leaves_ref, len_ref,
-    gq_ref, gks_ref, gvs_ref, gkp_ref, gvp_ref,
-    q, g, ks, vs, kp, vp, w_s, gp_s, p_half, ds_half, bias, stats, own, sbuf, rbuf,
-    in_sem, k_send, k_recv, v_send, v_recv, r_send, r_recv,
+    q_hbm, ks_hbm, vs_hbm, kp_hbm, vp_hbm, g_hbm, parents_hbm, leaves_hbm, len_hbm,
+    gq_out, gks_out, gvs_out, gkp_out, gvp_out,
+    q, g, ks, vs, kp, vp, w_s, gp_s, p_half, ds_half, bias, stats, own, sbuf, rbuf, xbuf,
+    gq_ref, gks_ref, gvs_ref, gkp_ref, gvp_ref, parents_ref, leaves_ref, len_ref,
+    in_sem, g_send, g_recv, r_send, r_recv, x_send, x_recv, out_sem,
 ):
     rows, width = q.shape
     heads = width // HD
@@ -49,41 +51,103 @@
     slots = n * local
     chunk = min(slots, 256)
     chunks = slots // chunk
+    part = group * HD
     me = lax.axis_index("dp")
-    peers = [lax.rem(me + j, n) for j in range(1, n)]
+    relay = n == 4
+    is_end = jnp.logical_or(me == 0, me == n - 1)
+    is_mid = jnp.logical_not(is_end)
+    across = n - 1 - me
+    opposite = lax.rem(me + 2, n)
+    beside = jnp.where(me == 0, 1, n - 2)
+    hops = [2, 1, 3] if relay else list(range(1, n))
+    peers = {j: lax.rem(me + j, n) for j in hops}
+    hcol = lambda h: slice(h * HD, (h + 1) * HD)
+    brow = lambda b: slice(b * SUF, (b + 1) * SUF)
+
+    def when(condition, action):
+        if condition is None:
+            action()
+        elif relay:
+            pl.when(condition)(action)
+
+    def direct(j):
+        if not relay or j == 2:
+            return None
+        return me != (n - 1 if j == 1 else 0)
+
+    def remote(src, dst, send, recv, device):
+        return pltpu.make_async_remote_copy(
+            src_ref=src, dst_ref=dst, send_sem=send, recv_sem=recv,
+            device_id={"dp": device}, device_id_type=MESH,
+        )
 
     barrier = pltpu.get_barrier_semaphore()
-    for peer in peers:
+    for peer in peers.values():
         pl.semaphore_signal(barrier, inc=1, device_id={"dp": peer}, device_id_type=MESH)
 
-    part = group * HD
+    places = lambda d: pl.ds(pl.multiple_of(d * local, local), local)
+    mine = places(me)
+    small = [
+        pltpu.make_async_copy(parents_hbm, parents_ref, in_sem.at[0]),
+        pltpu.make_async_copy(leaves_hbm, leaves_ref, in_sem.at[1]),
+        pltpu.make_async_copy(len_hbm, len_ref, in_sem.at[2]),
+    ]
     loads = [
-        pltpu.make_async_copy(ks_hbm, ks, in_sem.at[0]),
-        pltpu.make_async_copy(vs_hbm, vs, in_sem.at[1]),
+        pltpu.make_async_copy(ks_hbm, ks, in_sem.at[3]),
+        pltpu.make_async_copy(vs_hbm, vs, in_sem.at[4]),
     ]
     for m in range(kv):
         cols = pl.ds(m * part, part)
-        loads.append(pltpu.make_async_copy(q_hbm.at[:, cols], q.at[:, cols], in_sem.at[4 + 2 * m]))
-        loads.append(pltpu.make_async_copy(g_hbm.at[:, cols], g.at[:, cols], in_sem.at[5 + 2 * m]))
-    mine = pl.ds(pl.multiple_of(me * local, local), local)
-    own_copies = [
-        pltpu.make_async_copy(kp_hbm, kp.at[mine], in_sem.at[2]),
-        pltpu.make_async_copy(vp_hbm, vp.at[mine], in_sem.at[3]),
-    ]
-    for copy in loads + own_copies:
+        base = 5 + 4 * m
+        loads.append(pltpu.make_async_copy(q_hbm.at[:, cols], q.at[:, cols], in_sem.at[base]))
+        loads.append(pltpu.make_async_copy(g_hbm.at[:, cols], g.at[:, cols], in_sem.at[base + 1]))
+    own_copies = []
+    for m in range(kv):
+        for w, (src, dst) in enumerate(((kp_hbm, kp), (vp_hbm, vp))):
+            own_copies.append(
+                pltpu.make_async_copy(src.at[:, hcol(m)], dst.at[m, mine], in_sem.at[7 + 4 * m + w])
+            )
+    for copy in small + loads + own_copies:
         copy.start()
 
-    pl.semaphore_wait(barrier, n - 1)
-    gathers = []
-    for src, dst, send, recv in ((kp_hbm, kp, k_send, k_recv), (vp_hbm, vp, v_send, v_recv)):
-        for j, peer in enumerate(peers):
-            copy = pltpu.make_async_remote_copy(
-                src_ref=src, dst_ref=dst.at[mine], send_sem=send.at[j], recv_sem=recv.at[j],
-                device_id={"dp": peer}, device_id_type=MESH,
-            )
-            copy.start()
-            gathers.append(copy)
-
+    sent = []
+
+    def start(condition, copy):
+        when(condition, copy.start)
+        sent.append((condition, copy))
+
+    pl.semaphore_wait(barrier, len(hops))
+    for m in range(kv):
+        for w, (src, dst) in enumerate(((kp_hbm, kp), (vp_hbm, vp))):
+            for j in hops:
+                start(direct(j), remote(
+                    src.at[:, hcol(m)], dst.at[m, mine], g_send.at[m, w, j], g_recv.at[m, w, me],
+                    peers[j],
+                ))
+
+    def block_of(m, w, owner, device):
+        held = (kp, vp)[w].at[m, places(owner)]
+        return remote(held, held, g_send.at[m, w, 0], g_recv.at[m, w, owner], device)
+
+    def pass_on(m):
+        if relay:
+            for w in range(2):
+                block_of(m, w, opposite, across).wait_recv()
+                start(is_mid, block_of(m, w, opposite, n - 1 - opposite))
+
+    def wait_blocks(m):
+        for w in range(2):
+            for j in hops:
+                if not relay or j != 2:
+                    block_of(m, w, peers[j], peers[j]).wait_recv()
+
+    def clear():
+        rbuf[:, across] = jnp.zeros((kv,) + rbuf.shape[2:], rbuf.dtype)
+
+    if relay:
+        pl.when(is_end)(clear)
+    for copy in small:
+        copy.wait()
     nodes = len_ref.shape[0]
     place = lax.broadcasted_iota(jnp.int32, (BLK, SUF), 0)
     for b in range(nb):
@@ -99,8 +163,6 @@
     causal = lax.broadcasted_iota(jnp.int32, (SUF, SUF), 0) <= lax.broadcasted_iota(
         jnp.int32, (SUF, SUF), 1
     )
-    hcol = lambda h: slice(h * HD, (h + 1) * HD)
-    brow = lambda b: slice(b * SUF, (b + 1) * SUF)
 
     loads[0].wait()
     loads[1].wait()
@@ -121,15 +183,34 @@
             stats[h, 1:2, brow(b)] = jnp.sum(w, axis=0, keepdims=True)
             stats[h, 2:3, brow(b)] = jnp.sum(w * gp, axis=0, keepdims=True)
 
+    def partial_to(m, j):
+        return remote(
+            sbuf.at[m, peers[j]], rbuf.at[m, me], r_send.at[m, j], r_recv.at[m, me], peers[j]
+        )
+
+    def partial_from(m, owner):
+        return remote(sbuf.at[m, 0], rbuf.at[m, owner], r_send.at[m, 0], r_recv.at[m, owner], owner)
+
+    def combine(m):
+        def add():
+            remote(sbuf.at[m, 0], xbuf.at[m], x_send.at[m], x_recv.at[m], beside).wait_recv()
+            for w in range(2):
+                joint = own[m, w, places(opposite), :] + xbuf[m, w].astype(jnp.float32)
+                sbuf[m, opposite, w] = joint.astype(jnp.bfloat16)
+
+        if relay:
+            when(is_mid, add)
+            start(is_mid, partial_to(m, 2))
+
     for copy in own_copies:
         copy.wait()
-    for copy in gathers:
-        copy.wait_recv()
-
-    sends = []
-    for m in range(kv):
+    pass_on(0)
+    for m in range(kv):
+        wait_blocks(m)
         for i in range(group):
             h = m * group + i
+            if i == group // 2 and m + 1 < kv:
+                pass_on(m + 1)
 
             def at(c):
                 if chunks == 1:
@@ -137,10 +218,10 @@
                 return pl.ds(pl.multiple_of(c * chunk, chunk), chunk)
 
             def scores(c):
-                return dot_nt(kp[at(c), hcol(m)], q[:, hcol(h)]) + bias[at(c), :]
+                return dot_nt(kp[m, at(c), :], q[:, hcol(h)]) + bias[at(c), :]
 
             def grads(c):
-                return dot_nt(vp[at(c), hcol(m)], g[:, hcol(h)])
+                return dot_nt(vp[m, at(c), :], g[:, hcol(h)])
 
             if chunks == 1:
                 only_s, only_g = scores(0), grads(0)
@@ -204,17 +285,19 @@
                 put(at_d, d, grad_v[at_d], grad_k[at_d])
         else:
             lax.fori_loop(0, n, reduce_node, 0)
-        for j, peer in enumerate(peers):
-            copy = pltpu.make_async_remote_copy(
-                src_ref=sbuf.at[m, peer], dst_ref=rbuf.at[m, j],
-                send_sem=r_send.at[m, j], recv_sem=r_recv.at[m, j],
-                device_id={"dp": peer}, device_id_type=MESH,
-            )
-            copy.start()
-            sends.append(copy)
-
-    for m in range(kv):
-        kp_t = kp[:, hcol(m)].T
+        if relay:
+            start(is_end, remote(
+                sbuf.at[m, across], xbuf.at[m], x_send.at[m], x_recv.at[m], beside
+            ))
+        for j in hops:
+            condition = is_end if relay and j == 2 else direct(j)
+            start(condition, partial_to(m, j))
+        if m > 0:
+            combine(m - 1)
+
+    results = []
+    for m in range(kv):
+        kp_t = kp[m].T
         ks_t = [ks[brow(b), hcol(m)].T for b in range(nb)]
         p_parts = [[] for b in range(nb)]
         d_parts = [[] for b in range(nb)]
@@ -236,17 +319,53 @@
             grad_k = dot_nn(jnp.concatenate(d_parts[b], axis=1), q_all) * SCALE
             gks_ref[brow(b), hcol(m)] = grad_k.astype(jnp.bfloat16)
             gvs_ref[brow(b), hcol(m)] = grad_v.astype(jnp.bfloat16)
-
-    for copy in sends:
-        copy.wait_recv()
-    for m in range(kv):
-        for which, out in ((0, gkp_ref), (1, gvp_ref)):
-            summed = own[m, which, mine, :]
-            for j in range(n - 1):
-                summed = summed + rbuf[m, j, which].astype(jnp.float32)
+        cols = pl.ds(m * part, part)
+        results.append(
+            pltpu.make_async_copy(gq_ref.at[:, cols], gq_out.at[:, cols], out_sem.at[4 + m])
+        )
+        results[-1].start()
+        if m == kv - 1:
+            results.append(pltpu.make_async_copy(gks_ref, gks_out, out_sem.at[2]))
+            results.append(pltpu.make_async_copy(gvs_ref, gvs_out, out_sem.at[3]))
+            results[-2].start()
+            results[-1].start()
+
+    combine(kv - 1)
+    for m in range(kv):
+        for j in hops:
+            if not relay or j == 2:
+                condition = None
+            else:
+                condition = direct(j)
+            when(condition, partial_from(m, peers[j]).wait_recv)
+        for w, out in ((0, gkp_ref), (1, gvp_ref)):
+            summed = own[m, w, mine, :]
+            for j in hops:
+                summed = summed + rbuf[m, peers[j], w].astype(jnp.float32)
             out[:, hcol(m)] = summed.astype(jnp.bfloat16)
-    for copy in gathers + sends:
-        copy.wait_send()
+    last = [
+        pltpu.make_async_copy(gkp_ref, gkp_out, out_sem.at[0]),
+        pltpu.make_async_copy(gvp_ref, gvp_out, out_sem.at[1]),
+    ]
+    for copy in last:
+        copy.start()
+    for condition, copy in sent:
+        when(condition, copy.wait_send)
+    for copy in results + last:
+        copy.wait()
+
+
+def write_out(*refs):
+    sources, outs, held, sems = refs[:5], refs[5:10], refs[10:15], refs[15]
+    loads = [pltpu.make_async_copy(a, b, sems.at[0, i]) for i, (a, b) in enumerate(zip(sources, held))]
+    stores = [pltpu.make_async_copy(a, b, sems.at[1, i]) for i, (a, b) in enumerate(zip(held, outs))]
+    for copy in loads:
+        copy.start()
+    for load, store in zip(loads, stores):
+        load.wait()
+        store.start()
+    for copy in stores:
+        copy.wait()
 
 
 def body(n, queries, suffix_keys, suffix_values, prefix_keys, prefix_values, grad_out,
@@ -258,11 +377,9 @@
     local = prefix_keys.shape[0]
     slots = n * local
     half, full = jnp.bfloat16, jnp.float32
-    any_spec = pl.BlockSpec(memory_space=pl.ANY)
-    smem = pl.BlockSpec(memory_space=pltpu.SMEM)
-    vmem = pl.BlockSpec(memory_space=pltpu.VMEM)
+    hbm = pl.BlockSpec(memory_space=pl.ANY)
     flops = 10 * rows * heads * HD * (slots + SUF)
-    return pl.pallas_call(
+    results = pl.pallas_call(
         functools.partial(kernel, n),
         out_shape=(
             jax.ShapeDtypeStruct((rows, width), half),
@@ -271,15 +388,15 @@
             jax.ShapeDtypeStruct((local, kv_width), half),
             jax.ShapeDtypeStruct((local, kv_width), half),
         ),
-        in_specs=[any_spec] * 6 + [smem] * 3,
-        out_specs=(vmem,) * 5,
+        in_specs=[hbm] * 9,
+        out_specs=(hbm,) * 5,
         scratch_shapes=[
             pltpu.VMEM((rows, width), half),
             pltpu.VMEM((rows, width), half),
             pltpu.VMEM((rows, kv_width), half),
             pltpu.VMEM((rows, kv_width), half),
-            pltpu.VMEM((slots, kv_width), half),
-            pltpu.VMEM((slots, kv_width), half),
+            pltpu.VMEM((kv, slots, HD), half),
+            pltpu.VMEM((kv, slots, HD), half),
             pltpu.VMEM((heads, SUF, rows), full),
             pltpu.VMEM((heads, SUF, rows), full),
             pltpu.VMEM((kv, slots, group * rows), half),
@@ -288,23 +405,43 @@
             pltpu.VMEM((heads, 8, rows), full),
             pltpu.VMEM((kv, 2, slots, HD), full),
             pltpu.VMEM((kv, n, 2, local, HD), half),
-            pltpu.VMEM((kv, n - 1, 2, local, HD), half),
-            pltpu.SemaphoreType.DMA((4 + 2 * kv,)),
-            pltpu.SemaphoreType.DMA((n - 1,)),
-            pltpu.SemaphoreType.DMA((n - 1,)),
-            pltpu.SemaphoreType.DMA((n - 1,)),
-            pltpu.SemaphoreType.DMA((n - 1,)),
-            pltpu.SemaphoreType.DMA((kv, n - 1)),
-            pltpu.SemaphoreType.DMA((kv, n - 1)),
+            pltpu.VMEM((kv, n, 2, local, HD), half),
+            pltpu.VMEM((kv, 2, local, HD), half),
+            pltpu.VMEM((rows, width), half),
+            pltpu.VMEM((rows, kv_width), half),
+            pltpu.VMEM((rows, kv_width), half),
+            pltpu.VMEM((local, kv_width), half),
+            pltpu.VMEM((local, kv_width), half),
+            pltpu.SMEM(parents.shape, jnp.int32),
+            pltpu.SMEM(leaves.shape, jnp.int32),
+            pltpu.SMEM(node_len.shape, jnp.int32),
+            pltpu.SemaphoreType.DMA((5 + 4 * kv,)),
+            pltpu.SemaphoreType.DMA((kv, 2, n)),
+            pltpu.SemaphoreType.DMA((kv, 2, n)),
+            pltpu.SemaphoreType.DMA((kv, n)),
+            pltpu.SemaphoreType.DMA((kv, n)),
+            pltpu.SemaphoreType.DMA((kv,)),
+            pltpu.SemaphoreType.DMA((kv,)),
+            pltpu.SemaphoreType.DMA((4 + kv,)),
         ],
         compiler_params=pltpu.CompilerParams(
-            collective_id=0, has_side_effects=True, vmem_limit_bytes=48 * 1024 * 1024
+            collective_id=0, has_side_effects=True, vmem_limit_bytes=LIMIT
         ),
         cost_estimate=pl.CostEstimate(
             flops=flops, bytes_accessed=8 * rows * width, transcendentals=rows * heads * (slots + SUF)
         ),
     )(queries, suffix_keys, suffix_values, prefix_keys, prefix_values, grad_out,
       parents, leaves, node_len)
+    return pl.pallas_call(
+        write_out,
+        out_shape=tuple(jax.ShapeDtypeStruct(r.shape, r.dtype) for r in results),
+        in_specs=[pl.BlockSpec(memory_space=pl.ANY)] * 5,
+        out_specs=(hbm,) * 5,
+        scratch_shapes=[pltpu.VMEM(r.shape, r.dtype) for r in results]
+        + [pltpu.SemaphoreType.DMA((2, 5))],
+        compiler_params=pltpu.CompilerParams(vmem_limit_bytes=LIMIT),
+        cost_estimate=pl.CostEstimate(flops=0, bytes_accessed=4 * rows * width, transcendentals=0),
+    )(*results)
 
 
 def solution(mesh):

time: 31.7 us -> 25.4 us (0.80)
  local copies, waits for them, and re-layouts: 10.8 us -> 0 us
  Pallas kernels: 19.8 us -> 24.6 us
    unnamed x23 -> x0, local copies, waits for them, and re-layouts: 10.8 us -> none
    pallas_call x1, Pallas kernels: 19.8 us -> 22.5 us  [body(): pl.pallas_call(functools.partial(kernel, n), out_shape=(jax.ShapeDtypeStr...]
    pallas_call x0 -> x1, Pallas kernels: none -> 2.1 us  [body(): pl.pallas_call(write_out, out_shape=tuple((jax.ShapeDtypeStruct(r.shape,...]
where the time goes in v2:
time: 25.4 us; the launch traced here: 25.3 us
  Pallas kernels  24.6 us (97%)
  between operations  0.64 us (3%)
    pallas_call x1, Pallas kernels, body(): pl.pallas_call(functools.partial(kernel, n), out_shape=(jax.ShapeDtypeStr...  22.5 us
    pallas_call x1, Pallas kernels, body(): pl.pallas_call(write_out, out_shape=tuple((jax.ShapeDtypeStruct(r.shape,...  2.1 us

profile of v2, /device:TPU:0, one launch (start us, length us, event | category | flops | bytes accessed | tf_op | source)
XLA Modules:
  0.0 25.3 jit_solution(14231156950431975455)
XLA Ops:
  0.6 22.5 %shard_map.128 = (bf16[256,1280]{1,0:T(8,128)(2,1)}, bf16[256,256]{1,0:T(8,128)(2,1)}, bf16[256,256]{1,0:T(8,128)(2,1)}, bf16[64,256]{1,0:T(8,128)(2,1)}, bf16[64,256]{1,0:T(8,128)(2,1)}) custom-call(bf16[256,1280]{1,0:T(8,128)(2,1)} %q_hbm.1, bf16[256,256]{1,0:T(8,128)(2,1)} %ks_hbm.1, bf16[256,256]{1,0:T(8,128)(2,1)} %vs_hbm.1, bf16[64,256]{1,0:T(8,128)(2,1)} %kp_hbm.1, ...), custom_call_target="tpu_custom_call" | custom-call | flops 1258291200 | bytes 2621440 | tf_op jit(solution)/shard_map/pallas_call | solution.py:382
  23.2 2.1 %shard_map.129 = (bf16[256,1280]{1,0:T(8,128)(2,1)}, bf16[256,256]{1,0:T(8,128)(2,1)}, bf16[256,256]{1,0:T(8,128)(2,1)}, bf16[64,256]{1,0:T(8,128)(2,1)}, bf16[64,256]{1,0:T(8,128)(2,1)}) custom-call(bf16[256,1280]{1,0:T(8,128)(2,1)} %get-tuple-element.10.refs_0_, bf16[256,256]{1,0:T(8,128)(2,1)} %get-tuple-element.11.refs_1_, ...), custom_call_target="tpu_custom_call" | custom-call | bytes 1310720 | tf_op jit(solution)/shard_map/pallas_call | solution.py:435

commit v3 on v2

--- a/solution.py
+++ b/solution.py
@@ -38,9 +38,9 @@
     n,
     q_hbm, ks_hbm, vs_hbm, kp_hbm, vp_hbm, g_hbm, parents_hbm, leaves_hbm, len_hbm,
     gq_out, gks_out, gvs_out, gkp_out, gvp_out,
-    q, g, ks, vs, kp, vp, w_s, gp_s, p_half, ds_half, bias, stats, own, sbuf, rbuf, xbuf,
+    q, g, ks, vs, kp, vp, w_s, gp_s, p_half, ds_half, bias, stats, own, sbuf, rbuf,
     gq_ref, gks_ref, gvs_ref, gkp_ref, gvp_ref, parents_ref, leaves_ref, len_ref,
-    in_sem, g_send, g_recv, r_send, r_recv, x_send, x_recv, out_sem,
+    in_sem, g_send, g_recv, r_send, r_recv, out_sem,
 ):
     rows, width = q.shape
     heads = width // HD
@@ -53,27 +53,10 @@
     chunks = slots // chunk
     part = group * HD
     me = lax.axis_index("dp")
-    relay = n == 4
-    is_end = jnp.logical_or(me == 0, me == n - 1)
-    is_mid = jnp.logical_not(is_end)
-    across = n - 1 - me
-    opposite = lax.rem(me + 2, n)
-    beside = jnp.where(me == 0, 1, n - 2)
-    hops = [2, 1, 3] if relay else list(range(1, n))
+    hops = list(range(1, n))
     peers = {j: lax.rem(me + j, n) for j in hops}
     hcol = lambda h: slice(h * HD, (h + 1) * HD)
     brow = lambda b: slice(b * SUF, (b + 1) * SUF)
-
-    def when(condition, action):
-        if condition is None:
-            action()
-        elif relay:
-            pl.when(condition)(action)
-
-    def direct(j):
-        if not relay or j == 2:
-            return None
-        return me != (n - 1 if j == 1 else 0)
 
     def remote(src, dst, send, recv, device):
         return pltpu.make_async_remote_copy(
@@ -112,40 +95,28 @@
 
     sent = []
 
-    def start(condition, copy):
-        when(condition, copy.start)
-        sent.append((condition, copy))
+    def start(copy):
+        copy.start()
+        sent.append(copy)
 
     pl.semaphore_wait(barrier, len(hops))
     for m in range(kv):
         for w, (src, dst) in enumerate(((kp_hbm, kp), (vp_hbm, vp))):
             for j in hops:
-                start(direct(j), remote(
+                start(remote(
                     src.at[:, hcol(m)], dst.at[m, mine], g_send.at[m, w, j], g_recv.at[m, w, me],
                     peers[j],
                 ))
 
-    def block_of(m, w, owner, device):
+    def block_of(m, w, owner):
         held = (kp, vp)[w].at[m, places(owner)]
-        return remote(held, held, g_send.at[m, w, 0], g_recv.at[m, w, owner], device)
-
-    def pass_on(m):
-        if relay:
-            for w in range(2):
-                block_of(m, w, opposite, across).wait_recv()
-                start(is_mid, block_of(m, w, opposite, n - 1 - opposite))
+        return remote(held, held, g_send.at[m, w, 0], g_recv.at[m, w, owner], owner)
 
     def wait_blocks(m):
         for w in range(2):
             for j in hops:
-                if not relay or j != 2:
-                    block_of(m, w, peers[j], peers[j]).wait_recv()
-
-    def clear():
-        rbuf[:, across] = jnp.zeros((kv,) + rbuf.shape[2:], rbuf.dtype)
-
-    if relay:
-        pl.when(is_end)(clear)
+                block_of(m, w, peers[j]).wait_recv()
+
     for copy in small:
         copy.wait()
     nodes = len_ref.shape[0]
@@ -191,26 +162,12 @@
     def partial_from(m, owner):
         return remote(sbuf.at[m, 0], rbuf.at[m, owner], r_send.at[m, 0], r_recv.at[m, owner], owner)
 
-    def combine(m):
-        def add():
-            remote(sbuf.at[m, 0], xbuf.at[m], x_send.at[m], x_recv.at[m], beside).wait_recv()
-            for w in range(2):
-                joint = own[m, w, places(opposite), :] + xbuf[m, w].astype(jnp.float32)
-                sbuf[m, opposite, w] = joint.astype(jnp.bfloat16)
-
-        if relay:
-            when(is_mid, add)
-            start(is_mid, partial_to(m, 2))
-
     for copy in own_copies:
         copy.wait()
-    pass_on(0)
     for m in range(kv):
         wait_blocks(m)
         for i in range(group):
             h = m * group + i
-            if i == group // 2 and m + 1 < kv:
-                pass_on(m + 1)
 
             def at(c):
                 if chunks == 1:
@@ -285,15 +242,8 @@
                 put(at_d, d, grad_v[at_d], grad_k[at_d])
         else:
             lax.fori_loop(0, n, reduce_node, 0)
-        if relay:
-            start(is_end, remote(
-                sbuf.at[m, across], xbuf.at[m], x_send.at[m], x_recv.at[m], beside
-            ))
         for j in hops:
-            condition = is_end if relay and j == 2 else direct(j)
-            start(condition, partial_to(m, j))
-        if m > 0:
-            combine(m - 1)
+            start(partial_to(m, j))
 
     results = []
     for m in range(kv):
@@ -330,14 +280,9 @@
             results[-2].start()
             results[-1].start()
 
-    combine(kv - 1)
     for m in range(kv):
         for j in hops:
-            if not relay or j == 2:
-                condition = None
-            else:
-                condition = direct(j)
-            when(condition, partial_from(m, peers[j]).wait_recv)
+            partial_from(m, peers[j]).wait_recv()
         for w, out in ((0, gkp_ref), (1, gvp_ref)):
             summed = own[m, w, mine, :]
             for j in hops:
@@ -349,8 +294,8 @@
     ]
     for copy in last:
         copy.start()
-    for condition, copy in sent:
-        when(condition, copy.wait_send)
+    for copy in sent:
+        copy.wait_send()
     for copy in results + last:
         copy.wait()
 
@@ -406,7 +351,6 @@
             pltpu.VMEM((kv, 2, slots, HD), full),
             pltpu.VMEM((kv, n, 2, local, HD), half),
             pltpu.VMEM((kv, n, 2, local, HD), half),
-            pltpu.VMEM((kv, 2, local, HD), half),
             pltpu.VMEM((rows, width), half),
             pltpu.VMEM((rows, kv_width), half),
             pltpu.VMEM((rows, kv_width), half),
@@ -420,8 +364,6 @@
             pltpu.SemaphoreType.DMA((kv, 2, n)),
             pltpu.SemaphoreType.DMA((kv, n)),
             pltpu.SemaphoreType.DMA((kv, n)),
-            pltpu.SemaphoreType.DMA((kv,)),
-            pltpu.SemaphoreType.DMA((kv,)),
             pltpu.SemaphoreType.DMA((4 + kv,)),
         ],
         compiler_params=pltpu.CompilerParams(

time: 25.4 us -> 21.7 us (0.85)
  Pallas kernels: 24.6 us -> 20.9 us
    pallas_call x1, Pallas kernels: 22.5 us -> 18.8 us  [body(): pl.pallas_call(functools.partial(kernel, n), out_shape=(jax.ShapeDtypeStr...]
where the time goes in v3:
time: 21.7 us; the launch traced here: 21.5 us
  Pallas kernels  20.9 us (96%)
  between operations  0.64 us (3%)
    pallas_call x1, Pallas kernels, body(): pl.pallas_call(functools.partial(kernel, n), out_shape=(jax.ShapeDtypeStr...  18.8 us
    pallas_call x1, Pallas kernels, body(): pl.pallas_call(write_out, out_shape=tuple((jax.ShapeDtypeStruct(r.shape,...  2.1 us

profile of v3, /device:TPU:0, one launch (start us, length us, event | category | flops | bytes accessed | tf_op | source)
XLA Modules:
  0.0 21.5 jit_solution(16988517449418091101)
XLA Ops:
  0.6 18.8 %shard_map.128 = (bf16[256,1280]{1,0:T(8,128)(2,1)}, bf16[256,256]{1,0:T(8,128)(2,1)}, bf16[256,256]{1,0:T(8,128)(2,1)}, bf16[64,256]{1,0:T(8,128)(2,1)}, bf16[64,256]{1,0:T(8,128)(2,1)}) custom-call(bf16[256,1280]{1,0:T(8,128)(2,1)} %q_hbm.1, bf16[256,256]{1,0:T(8,128)(2,1)} %ks_hbm.1, bf16[256,256]{1,0:T(8,128)(2,1)} %vs_hbm.1, bf16[64,256]{1,0:T(8,128)(2,1)} %kp_hbm.1, ...), custom_call_target="tpu_custom_call" | custom-call | flops 1258291200 | bytes 2621440 | tf_op jit(solution)/shard_map/pallas_call | solution.py:327
  19.4 2.1 %shard_map.129 = (bf16[256,1280]{1,0:T(8,128)(2,1)}, bf16[256,256]{1,0:T(8,128)(2,1)}, bf16[256,256]{1,0:T(8,128)(2,1)}, bf16[64,256]{1,0:T(8,128)(2,1)}, bf16[64,256]{1,0:T(8,128)(2,1)}) custom-call(bf16[256,1280]{1,0:T(8,128)(2,1)} %get-tuple-element.10.refs_0_, bf16[256,256]{1,0:T(8,128)(2,1)} %get-tuple-element.11.refs_1_, ...), custom_call_target="tpu_custom_call" | custom-call | bytes 1310720 | tf_op jit(solution)/shard_map/pallas_call | solution.py:377

commit v4 on v3

--- a/solution.py
+++ b/solution.py
@@ -54,7 +54,10 @@
     part = group * HD
     me = lax.axis_index("dp")
     hops = list(range(1, n))
-    peers = {j: lax.rem(me + j, n) for j in hops}
+    low = me < n // 2
+    rising = {j: jnp.where(j <= me, j - 1, j) for j in hops}
+    falling = {j: jnp.where(n - j > me, n - j, n - 1 - j) for j in hops}
+    peers = {j: jnp.where(low, falling[j], rising[j]) for j in hops}
     hcol = lambda h: slice(h * HD, (h + 1) * HD)
     brow = lambda b: slice(b * SUF, (b + 1) * SUF)
 

time: 21.7 us -> 21.5 us (level)
  no operation moved by 1% of the time
where the time goes in v4:
time: 21.5 us; the launch traced here: 21.4 us
  Pallas kernels  20.7 us (96%)
  between operations  0.64 us (3%)
    pallas_call x1, Pallas kernels, body(): pl.pallas_call(functools.partial(kernel, n), out_shape=(jax.ShapeDtypeStr...  18.6 us
    pallas_call x1, Pallas kernels, body(): pl.pallas_call(write_out, out_shape=tuple((jax.ShapeDtypeStruct(r.shape,...  2.1 us

profile of v4, /device:TPU:0, one launch (start us, length us, event | category | flops | bytes accessed | tf_op | source)
XLA Modules:
  0.0 21.4 jit_solution(12235997725642654346)
XLA Ops:
  0.6 18.6 %shard_map.128 = (bf16[256,1280]{1,0:T(8,128)(2,1)}, bf16[256,256]{1,0:T(8,128)(2,1)}, bf16[256,256]{1,0:T(8,128)(2,1)}, bf16[64,256]{1,0:T(8,128)(2,1)}, bf16[64,256]{1,0:T(8,128)(2,1)}) custom-call(bf16[256,1280]{1,0:T(8,128)(2,1)} %q_hbm.1, bf16[256,256]{1,0:T(8,128)(2,1)} %ks_hbm.1, bf16[256,256]{1,0:T(8,128)(2,1)} %vs_hbm.1, bf16[64,256]{1,0:T(8,128)(2,1)} %kp_hbm.1, ...), custom_call_target="tpu_custom_call" | custom-call | flops 1258291200 | bytes 2621440 | tf_op jit(solution)/shard_map/pallas_call | solution.py:330
  19.3 2.1 %shard_map.129 = (bf16[256,1280]{1,0:T(8,128)(2,1)}, bf16[256,256]{1,0:T(8,128)(2,1)}, bf16[256,256]{1,0:T(8,128)(2,1)}, bf16[64,256]{1,0:T(8,128)(2,1)}, bf16[64,256]{1,0:T(8,128)(2,1)}) custom-call(bf16[256,1280]{1,0:T(8,128)(2,1)} %get-tuple-element.10.refs_0_, bf16[256,256]{1,0:T(8,128)(2,1)} %get-tuple-element.11.refs_1_, ...), custom_call_target="tpu_custom_call" | custom-call | bytes 1310720 | tf_op jit(solution)/shard_map/pallas_call | solution.py:380
